TPU v7x, 32 devices: a whole 2x2x4 slice. The times are simulated.
32 devices in a mesh: grp: 2 (over y), ctx: 8 (over z, x), ch: 2 (over core).
Axes of the slice: x: 2, y: 2, z: 4, core: 2. Of those that a mesh axis runs over, the one named last changes fastest.
Arguments:
- qkv: bfloat16 [2048, 3, 8192], P(('grp', 'ctx'), None, 'ch'), parts along dimension 0, may hold values from -6 to 6
- g_out: bfloat16 [2048, 8192], P(('grp', 'ctx'), 'ch'), parts along dimension 0, may hold values from -6 to 6
- residue: float32 [512, 16], P('ch'), may hold values from -0.26 to 0.26
- decay: float32 [512, 16], P('ch'), may hold values from 9.765625e-05 to 0.034
Outputs:
- output: bfloat16 [2048, 8192], P(('grp', 'ctx'), 'ch'), parts along dimension 0
- grad_qkv: bfloat16 [2048, 3, 8192], P(('grp', 'ctx'), None, 'ch'), parts along dimension 0
- grad_res: float32 [1024, 16], P(('grp', 'ch')), parts along dimension 0
There are 2 independent parts, one for each index of `grp`. A program takes and returns all parts, laid end to end along the dimension named above; an argument that names none is the same for every part. Nothing has to cross between parts.
All inputs are finite; a program needn't handle non-finite values.
Results may differ from a plain program's by a relative error of at most 0.005.
Values sent between devices are 32-bit elements; how exact they have to be, the bound alone decides.
A program may use at most 128 MiB of HBM per device.

v0:
```python
import functools
import jax
import jax.numpy as jnp
from jax import lax
from jax.experimental import pallas as pl
from jax.experimental.pallas import tpu as pltpu
from jax.sharding import PartitionSpec as P

GROUP = 16
ORDER = 16
LANES = 256
PER = LANES // GROUP
ROWS = PER * ORDER
bf16 = jnp.bfloat16
f32 = jnp.float32
PAIR = 2


def split(a):
    hi = a.astype(bf16)
    return hi, (a - hi.astype(f32)).astype(bf16)


def mm(a, b, ca=1, cb=0):
    return lax.dot_general(a, b, (((ca,), (cb,)), ((), ())), preferred_element_type=f32)


def mm3(a, b, ca=1, cb=0):
    ah, al = split(a)
    bh, bl = split(b)
    return mm(ah, bh, ca, cb) + (mm(ah, bl, ca, cb) + mm(al, bh, ca, cb))


def iota(shape, dim):
    return lax.broadcasted_iota(jnp.int32, shape, dim)


def kernel(
    n, nb, per_chunk, length,
    q_ref, k_ref, v_ref, g_ref, d_ref, r_ref, drep_ref,
    out_ref, dq_ref, dk_ref, dv_ref, gr_ref,
    sig, cot, w0, w1, mix, gsig, own, peer, zf_in, zf_out, zb_in, zb_out, lags, gr_own, gr_all,
    xs, xr, fs, fr, bs, br, gs, grs,
):
    me = lax.axis_index("ctx")
    side = lax.rem(me, PAIR)
    z = me // PAIR
    nz = n // PAIR
    nc = nb // per_chunk
    partner = me + 1 - 2 * side
    half = 128

    barrier = pltpu.get_barrier_semaphore()

    def greet(i, c):
        pl.semaphore_signal(barrier, inc=1, device_id={"ctx": lax.rem(me + i, n)}, device_id_type=pl.DeviceIdType.MESH)
        return c

    lax.fori_loop(1, n, greet, 0)

    diag = (iota((ROWS, LANES), 0) // ORDER) == (iota((ROWS, LANES), 1) // GROUP)

    def states(j, c):
        cols = pl.ds(pl.multiple_of(j * LANES, LANES), LANES)
        sg = (k_ref[:, cols].astype(f32) * v_ref[:, cols].astype(f32)).astype(bf16)
        ct = (g_ref[:, cols].astype(f32) * q_ref[:, cols].astype(f32)).astype(bf16)
        sig[:, cols] = sg
        cot[:, cols] = ct
        d = d_ref[j]
        t = iota((length, LANES), 0).astype(f32)
        a0 = jnp.exp(-d * t)
        a1 = jnp.exp(-d * (length - t))
        w0[:, cols] = a0
        w1[:, cols] = a1
        for which, (a, x) in enumerate(((a1, sg), (a0, ct))):
            hi, lo = split(a.T)
            full = mm(hi, x) + mm(lo, x)
            own[j, which] = jnp.sum(jnp.where(diag, full, 0.0).reshape(PER, ORDER, LANES), axis=0)
        return c

    def xcopy(i):
        rows = pl.ds(i * per_chunk, per_chunk)
        return pltpu.make_async_remote_copy(
            src_ref=own.at[rows], dst_ref=peer.at[rows], send_sem=xs.at[i], recv_sem=xr.at[i],
            device_id={"ctx": partner}, device_id_type=pl.DeviceIdType.MESH)

    def zcopy(i, up):
        rows = pl.ds(i * per_chunk, per_chunk)
        src, dst, s, r = (zf_out, zf_in, fs, fr) if up else (zb_out, zb_in, bs, br)
        to = lax.rem(me + PAIR, n) if up else lax.rem(me + n - PAIR, n)
        return pltpu.make_async_remote_copy(
            src_ref=src.at[rows], dst_ref=dst.at[rows], send_sem=s.at[i], recv_sem=r.at[i],
            device_id={"ctx": to}, device_id_type=pl.DeviceIdType.MESH)

    def first(i, c):
        for u in range(per_chunk):
            states(i * per_chunk + u, 0)
        xcopy(i).start()
        return c

    pl.semaphore_wait(barrier, n - 1)
    lax.fori_loop(0, nc, first, 0)

    def fade(j):
        return jnp.exp(-drep_ref[:, pl.ds(pl.multiple_of(j * LANES, LANES), LANES)] * float(length))

    lower = iota((length, length), 1) <= iota((length, length), 0)
    upper = iota((length, length), 1) >= iota((length, length), 0)
    across = iota((length, length), 0) + iota((length, length), 1)
    corner = across <= length - 1
    flip = jnp.where(across == length - 1, 1.0, 0.0).astype(bf16)
    pick = (iota((PER, ROWS), 1) // ORDER) == iota((PER, ROWS), 0)
    pick16 = jnp.where(pick, 1.0, 0.0).astype(bf16)

    def heavy(j):
        cols = pl.ds(pl.multiple_of(j * LANES, LANES), LANES)
        r = r_ref[j]
        a0 = w0[:, cols]
        a1 = w1[:, cols]
        row0 = iota((length, LANES), 0) == 0
        h0, l0 = split(r * a0)
        h1, l1 = split(r * jnp.where(row0, 1.0, a1))
        h = mm(pick16, h0, 1, 1) + mm(pick16, l0, 1, 1)
        hr = mm(pick16, h1, 1, 1) + mm(pick16, l1, 1, 1)
        for p in range(LANES // half):
            hc = pl.ds(pl.multiple_of(j * LANES + p * half, half), half)
            sg = sig[:, hc]
            ct = cot[:, hc]
            back = mm(flip, ct)
            lane_group = iota((length, half), 1) // GROUP
            macc = jnp.zeros((length, half), f32)
            gacc = jnp.zeros((length, half), f32)
            for e in range(half // GROUP):
                g = p * (half // GROUP) + e
                tt = pltpu.roll(jnp.broadcast_to(h[g:g + 1], (length, length)), 0, 1, stride=1, stride_axis=0)
                tt = jnp.where(upper, tt, 0.0).astype(bf16)
                gacc = jnp.where(lane_group == e, mm(tt, ct), gacc)
                tf = pltpu.roll(jnp.broadcast_to(hr[g:g + 1], (length, length)), 0, 1, stride=1, stride_axis=0)
                tf = jnp.where(lower, tf, 0.0).astype(bf16)
                macc = jnp.where(lane_group == e, mm(tf, sg), macc)
                cm = jnp.where(lane_group == e, back, 0.0).astype(bf16)
                m = jnp.where(corner, mm(cm, sg, 1, 1), 0.0)
                m = pltpu.roll(m, 0, 1, stride=1, stride_axis=0)
                lags[g:g + 1, :] = jnp.sum(m, axis=0, keepdims=True)
            mix[:, hc] = macc
            gsig[:, hc] = gacc
        full = mm3(lags[...], jnp.exp(-d_ref[j] * (length - 1 - iota((length, LANES), 0)).astype(f32)))
        gr_own[pl.ds(j, 1)] = jnp.sum(jnp.where(pick, full, 0.0), axis=0, keepdims=True).reshape(1, 1, LANES)

    steps = max(nb, nc + nz)

    def comm(step):
        i = step - z

        @pl.when((i >= 0) & (i < nc))
        def _():
            @pl.when(z > 0)
            def _():
                zcopy(i, True).wait_recv()

            @pl.when(z < nz - 1)
            def _():
                for u in range(per_chunk):
                    j = i * per_chunk + u
                    f = fade(j)
                    mine, other = own[j, 0], peer[j, 0]
                    pair = jnp.where(side == 0, f * mine + other, f * other + mine)
                    zf_out[j] = pair + jnp.where(z > 0, f * f * zf_in[j], 0.0)
                zcopy(i, True).start()

        i2 = step - (nz - 1 - z)

        @pl.when((i2 >= 0) & (i2 < nc))
        def _():
            @pl.when(z < nz - 1)
            def _():
                zcopy(i2, False).wait_recv()

            @pl.when(z > 0)
            def _():
                for u in range(per_chunk):
                    j = i2 * per_chunk + u
                    f = fade(j)
                    mine, other = own[j, 1], peer[j, 1]
                    pair = jnp.where(side == 0, mine + f * other, other + f * mine)
                    zb_out[j] = pair + jnp.where(z < nz - 1, f * f * zb_in[j], 0.0)
                zcopy(i2, False).start()

    @pl.when(z == 0)
    def _():
        zf_in[...] = jnp.zeros_like(zf_in)

    @pl.when(z == nz - 1)
    def _():
        zb_in[...] = jnp.zeros_like(zb_in)

    def second(s, c):
        @pl.when(s < nb)
        def _():
            heavy(s)

        @pl.when((s >= 1) & (s - 1 < nc))
        def _():
            xcopy(s - 1).wait_recv()

        @pl.when(s >= 1)
        def _():
            comm(s - 1)

        return c

    lax.fori_loop(0, steps, second, 0)

    def carries(j, c):
        f = fade(j)
        zf, zb = zf_in[j], zb_in[j]
        cf = jnp.where(side == 0, zf, f * zf + peer[j, 0])
        cb = jnp.where(side == 0, f * zb + peer[j, 1], zb)
        zf_in[j] = cf
        zb_in[j] = cb
        hi, lo = split(own[j, 1] * cf)
        cross = mm(hi, pick16, 1, 1) + mm(lo, pick16, 1, 1)
        gr_own[nb + j] = fold(cross)
        return c

    def fold(cross):
        spread = mm3(cross, jnp.where(pick, 1.0, 0.0))
        keep = lax.rem(iota((ORDER, ROWS), 1), ORDER) == iota((ORDER, ROWS), 0)
        return jnp.sum(jnp.where(keep, spread, 0.0), axis=0, keepdims=True)

    lax.fori_loop(0, nb, carries, 0)

    def gcopy(i):
        to = lax.rem(me + i, n)
        return pltpu.make_async_remote_copy(
            src_ref=gr_own, dst_ref=gr_all.at[i], send_sem=gs.at[i], recv_sem=grs.at[i],
            device_id={"ctx": to}, device_id_type=pl.DeviceIdType.MESH)

    def gstart(i, c):
        gcopy(i).start()
        return c

    lax.fori_loop(1, n, gstart, 0)

    def last(j, c):
        cols = pl.ds(pl.multiple_of(j * LANES, LANES), LANES)
        r = r_ref[j]
        cf = jnp.where(diag, jnp.concatenate([zf_in[j]] * PER, 0), 0.0)
        cb = jnp.where(diag, jnp.concatenate([zb_in[j]] * PER, 0), 0.0)
        m = mix[:, cols] + mm3(r * w0[:, cols], cf)
        gsv = gsig[:, cols] + mm3(r * w1[:, cols], cb)
        out_ref[:, cols] = (q_ref[:, cols].astype(f32) * m).astype(bf16)
        dq_ref[:, cols] = (g_ref[:, cols].astype(f32) * m).astype(bf16)
        dk_ref[:, cols] = (gsv * v_ref[:, cols].astype(f32)).astype(bf16)
        dv_ref[:, cols] = (gsv * k_ref[:, cols].astype(f32)).astype(bf16)
        return c

    lax.fori_loop(0, nb, last, 0)

    def xend(i, c):
        xcopy(i).wait_send()

        @pl.when(z < nz - 1)
        def _():
            zcopy(i, True).wait_send()

        @pl.when(z > 0)
        def _():
            zcopy(i, False).wait_send()

        return c

    lax.fori_loop(0, nc, xend, 0)

    def gend(i, c):
        gcopy(i).wait()
        return c

    lax.fori_loop(1, n, gend, 0)

    def gsum(i, acc):
        return acc + gr_all[i]

    gr_ref[...] = lax.fori_loop(1, n, gsum, gr_own[...])


def on_device(n, qkv, g_out, residue, decay):
    length, _, channels = qkv.shape
    nb = channels // LANES
    per_chunk = 2
    nc = nb // per_chunk
    q, k, v = qkv[:, 0], qkv[:, 1], qkv[:, 2]
    d_row = decay.reshape(nb, 1, ROWS)
    r_row = residue.reshape(nb, 1, ROWS)
    drep = jnp.repeat(decay.T, GROUP, axis=1)
    wide = jax.ShapeDtypeStruct((length, channels), bf16)
    vm = pl.BlockSpec(memory_space=pltpu.VMEM)
    dma = pltpu.SemaphoreType.DMA
    out, dq, dk, dv, gr = pl.pallas_call(
        functools.partial(kernel, n, nb, per_chunk, length),
        out_shape=(wide, wide, wide, wide, jax.ShapeDtypeStruct((2 * nb, 1, ROWS), f32)),
        in_specs=[vm] * 7,
        out_specs=(vm,) * 5,
        scratch_shapes=[
            pltpu.VMEM((length, channels), bf16),
            pltpu.VMEM((length, channels), bf16),
            pltpu.VMEM((length, channels), f32),
            pltpu.VMEM((length, channels), f32),
            pltpu.VMEM((length, channels), f32),
            pltpu.VMEM((length, channels), f32),
            pltpu.VMEM((nb, 2, ORDER, LANES), f32),
            pltpu.VMEM((nb, 2, ORDER, LANES), f32),
            pltpu.VMEM((nb, ORDER, LANES), f32),
            pltpu.VMEM((nb, ORDER, LANES), f32),
            pltpu.VMEM((nb, ORDER, LANES), f32),
            pltpu.VMEM((nb, ORDER, LANES), f32),
            pltpu.VMEM((PER, length), f32),
            pltpu.VMEM((2 * nb, 1, ROWS), f32),
            pltpu.VMEM((n, 2 * nb, 1, ROWS), f32),
            dma((nc,)), dma((nc,)), dma((nc,)), dma((nc,)), dma((nc,)), dma((nc,)),
            dma((n,)), dma((n,)),
        ],
        compiler_params=pltpu.CompilerParams(
            collective_id=0, has_side_effects=True, vmem_limit_bytes=56 * 1024 * 1024),
    )(q, k, v, g_out, d_row, r_row, drep)
    grad_res = (gr[:nb] + gr[nb:]).reshape(nb * PER, ORDER)
    return out, jnp.stack([dq, dk, dv], 1), grad_res


def solution(mesh):
    return jax.shard_map(
        functools.partial(on_device, mesh.shape["ctx"]),
        mesh=mesh,
        in_specs=(
            P(("grp", "ctx"), None, "ch"),
            P(("grp", "ctx"), "ch"),
            P("ch", None),
            P("ch", None),
        ),
        out_specs=(P(("grp", "ctx"), "ch"), P(("grp", "ctx"), None, "ch"), P(("grp", "ch"), None)),
        check_vma=False,
    )
```

profile of v0, /device:TPU:0, one launch (start us, length us, event | category | flops | bytes accessed | tf_op | source)
XLA Modules:
  0.0 76.9 jit_solution(11171329155440278846)
XLA Ops:
  0.6 0.8 %copy.11 = f32[256,16]{1,0:T(8,128)S(1)} copy(f32[256,16]{0,1:T(8,128)} %param.6) | data formatting | bytes 32768 | tf_op args[2]
  1.4 0.7 reshape.23.r_ref
  2.2 0.8 %copy.10 = f32[256,16]{1,0:T(8,128)S(1)} copy(f32[256,16]{0,1:T(8,128)} %param.7) | data formatting | bytes 32768 | tf_op args[3]
  3.0 0.7 reshape.22.d_ref
  3.7 1.3 %broadcast_in_dim.3 = f32[16,256,16]{2,1,0:T(8,128)S(1)} broadcast(f32[16,256]{1,0:T(8,128)} %bitcast.13), dimensions={0,1} | broadcast | bytes 278528 | tf_op jit(solution)/shard_map/broadcast_in_dim | solution.py:295
  5.0 2.3 %reshape.20.drep_ref = f32[16,4096]{1,0:T(8,128)} reshape(f32[16,256,16]{2,1,0:T(8,128)S(1)} %broadcast_in_dim.3) | data formatting | bytes 524288 | tf_op jit(solution)/shard_map/reshape | solution.py:295
  7.3 3.6 %slice_bitcast_fusion = (bf16[128,4096]{1,0:T(8,128)(2,1)}, bf16[128,4096]{1,0:T(8,128)(2,1)}, bf16[128,4096]{1,0:T(8,128)(2,1)}) fusion(bf16[128,3,4096]{2,0,1:T(8,128)(2,1)} %param.4), kind=kLoop, calls=%fused_computation.1 | loop fusion | bytes 6291456 | tf_op jit(solution)/shard_map/squeeze | solution.py:292
  10.9 60.2 %shard_map.67 = (bf16[128,4096]{1,0:T(8,128)(2,1)}, bf16[128,4096]{1,0:T(8,128)(2,1)}, bf16[128,4096]{1,0:T(8,128)(2,1)}, bf16[128,4096]{1,0:T(8,128)(2,1)}, f32[32,1,256]{2,1,0:T(1,128)}) custom-call(bf16[128,4096]{1,0:T(8,128)(2,1)} %get-tuple-element.20.q_ref, bf16[128,4096]{1,0:T(8,128)(2,1)} %get-tuple-element.21.k_ref, ...), custom_call_target="tpu_custom_call" | custom-call | tf_op jit(solution)/shard_map/pallas_call | solution.py:299
  71.1 0.0 copy-start.1
  71.1 0.0 copy-start
  71.1 3.9 %pad_maximum_fusion = bf16[128,3,4096]{2,0,1:T(8,128)(2,1)} fusion(bf16[128,1,4096]{2,0,1:T(8,128)(2,1)} %bitcast.12, bf16[128,1,4096]{2,0,1:T(8,128)(2,1)} %bitcast.11, bf16[128,1,4096]{2,0,1:T(8,128)(2,1)} %bitcast.10), kind=kLoop, calls=%fused_computation | loop fusion | flops 3145728 | bytes 6291456 | tf_op jit(solution)/shard_map/stack | solution.py:327
  75.1 0.0 copy-done.1
  75.1 0.1 reshape.21
  75.2 0.7 copy.14
  75.9 0.0 copy-done
  75.9 1.0 %copy.16 = bf16[128,4096]{1,0:T(8,128)(2,1)} copy(bf16[128,4096]{1,0:T(8,128)(2,1)S(1)} %copy-done) | data formatting | bytes 2097152
  (1 shorter events, 0.0 us)
Async XLA Ops:
  71.1 4.0 %copy-start.1 = (f32[32,1,256]{2,1,0:T(1,128)S(1)}, f32[32,1,256]{2,1,0:T(1,128)}, u32[]{:S(2)}) copy-start(f32[32,1,256]{2,1,0:T(1,128)} %get-tuple-element.12) | copy-start | bytes 98308
  71.1 4.8 %copy-start = (bf16[128,4096]{1,0:T(8,128)(2,1)S(1)}, bf16[128,4096]{1,0:T(8,128)(2,1)}, u32[]{:S(2)}) copy-start(bf16[128,4096]{1,0:T(8,128)(2,1)} %get-tuple-element.25) | copy-start | bytes 3145732
where the time goes:
time: 77.3 us; the launch traced here: 76.9 us
  Pallas kernels  60.2 us (78%)
  local copies, waits for them, and re-layouts  12 us (16%)
  other arithmetic  3.99 us (5%)
    pallas_call x1, Pallas kernels, on_device(): pl.pallas_call(functools.partial(kernel, n, nb, per_chunk, length), out_s...  60.2 us
    another operation x1, other arithmetic, on_device(): return (out, jnp.stack([dq, dk, dv], 1), grad_res)  3.95 us
    squeeze x1, local copies, waits for them, and re-layouts, on_device(): q, k, v = (qkv[:, 0], qkv[:, 1], qkv[:, 2])  3.62 us
    unnamed x8, local copies, waits for them, and re-layouts  3.29 us
    reshape x1, local copies, waits for them, and re-layouts, on_device(): drep = jnp.repeat(decay.T, GROUP, axis=1)  2.27 us

commit v1 on v0

--- a/solution.py
+++ b/solution.py
@@ -37,9 +37,9 @@
 
 def kernel(
     n, nb, per_chunk, length,
-    q_ref, k_ref, v_ref, g_ref, d_ref, r_ref, drep_ref,
-    out_ref, dq_ref, dk_ref, dv_ref, gr_ref,
-    sig, cot, w0, w1, mix, gsig, own, peer, zf_in, zf_out, zb_in, zb_out, lags, gr_own, gr_all,
+    x_ref, g_ref, dt_ref, rt_ref,
+    out_ref, dx_ref, gr_ref,
+    sig, cot, w0, w1, mix, gsig, own, peer, zf_in, zf_out, zb_in, zb_out, lags, gr_own, gr_all, drep, d_row, r_row, own_row, tmat,
     xs, xr, fs, fr, bs, br, gs, grs,
 ):
     me = lax.axis_index("ctx")
@@ -60,13 +60,31 @@
 
     diag = (iota((ROWS, LANES), 0) // ORDER) == (iota((ROWS, LANES), 1) // GROUP)
 
+    def chosen(j):
+        groups = nb * PER
+        hit = iota((groups, LANES), 0) == j * PER + iota((groups, LANES), 1) // GROUP
+        return jnp.where(hit, 1.0, 0.0).astype(bf16)
+
+    def spread(table, j):
+        hi = table.astype(bf16)
+        rest = table - hi.astype(f32)
+        mid = rest.astype(bf16)
+        low = (rest - mid.astype(f32)).astype(bf16)
+        hot = chosen(j)
+        return mm(hi, hot) + mm(mid, hot) + mm(low, hot)
+
     def states(j, c):
         cols = pl.ds(pl.multiple_of(j * LANES, LANES), LANES)
-        sg = (k_ref[:, cols].astype(f32) * v_ref[:, cols].astype(f32)).astype(bf16)
-        ct = (g_ref[:, cols].astype(f32) * q_ref[:, cols].astype(f32)).astype(bf16)
+        sg = (x_ref[1, :, cols].astype(f32) * x_ref[2, :, cols].astype(f32)).astype(bf16)
+        ct = (g_ref[:, cols].astype(f32) * x_ref[0, :, cols].astype(f32)).astype(bf16)
         sig[:, cols] = sg
         cot[:, cols] = ct
-        d = d_ref[j]
+        wide = spread(dt_ref[...], j)
+        own_mode = lax.rem(iota((ORDER, LANES), 1), ORDER) == iota((ORDER, LANES), 0)
+        drep[j] = jnp.exp(-wide * float(length))
+        d = jnp.sum(jnp.where(own_mode, wide, 0.0), axis=0, keepdims=True)
+        d_row[j] = d
+        r_row[j] = jnp.sum(jnp.where(own_mode, spread(rt_ref[...], j), 0.0), axis=0, keepdims=True)
         t = iota((length, LANES), 0).astype(f32)
         a0 = jnp.exp(-d * t)
         a1 = jnp.exp(-d * (length - t))
@@ -102,7 +120,7 @@
     lax.fori_loop(0, nc, first, 0)
 
     def fade(j):
-        return jnp.exp(-drep_ref[:, pl.ds(pl.multiple_of(j * LANES, LANES), LANES)] * float(length))
+        return drep[j]
 
     lower = iota((length, length), 1) <= iota((length, length), 0)
     upper = iota((length, length), 1) >= iota((length, length), 0)
@@ -114,7 +132,7 @@
 
     def heavy(j):
         cols = pl.ds(pl.multiple_of(j * LANES, LANES), LANES)
-        r = r_ref[j]
+        r = r_row[j]
         a0 = w0[:, cols]
         a1 = w1[:, cols]
         row0 = iota((length, LANES), 0) == 0
@@ -128,24 +146,32 @@
             ct = cot[:, hc]
             back = mm(flip, ct)
             lane_group = iota((length, half), 1) // GROUP
-            macc = jnp.zeros((length, half), f32)
-            gacc = jnp.zeros((length, half), f32)
+            back16 = back.astype(bf16)
             for e in range(half // GROUP):
                 g = p * (half // GROUP) + e
+                rows = pl.ds(e * length, length)
                 tt = pltpu.roll(jnp.broadcast_to(h[g:g + 1], (length, length)), 0, 1, stride=1, stride_axis=0)
-                tt = jnp.where(upper, tt, 0.0).astype(bf16)
-                gacc = jnp.where(lane_group == e, mm(tt, ct), gacc)
+                tmat[0, rows] = jnp.where(upper, tt, 0.0).astype(bf16)
                 tf = pltpu.roll(jnp.broadcast_to(hr[g:g + 1], (length, length)), 0, 1, stride=1, stride_axis=0)
-                tf = jnp.where(lower, tf, 0.0).astype(bf16)
-                macc = jnp.where(lane_group == e, mm(tf, sg), macc)
-                cm = jnp.where(lane_group == e, back, 0.0).astype(bf16)
-                m = jnp.where(corner, mm(cm, sg, 1, 1), 0.0)
-                m = pltpu.roll(m, 0, 1, stride=1, stride_axis=0)
+                tmat[1, rows] = jnp.where(lower, tf, 0.0).astype(bf16)
+                tmat[2, rows] = back16 * jnp.where(iota((1, half), 1) // GROUP == e, 1.0, 0.0).astype(bf16)
+            gall = mm(tmat[0], ct)
+            mall = mm(tmat[1], sg)
+            pall = mm(tmat[2], sg, 1, 1)
+            gacc = gall[:length]
+            macc = mall[:length]
+            for e in range(half // GROUP):
+                g = p * (half // GROUP) + e
+                at = slice(e * length, (e + 1) * length)
+                if e:
+                    gacc = jnp.where(lane_group == e, gall[at], gacc)
+                    macc = jnp.where(lane_group == e, mall[at], macc)
+                m = pltpu.roll(jnp.where(corner, pall[at], 0.0), 0, 1, stride=1, stride_axis=0)
                 lags[g:g + 1, :] = jnp.sum(m, axis=0, keepdims=True)
             mix[:, hc] = macc
             gsig[:, hc] = gacc
-        full = mm3(lags[...], jnp.exp(-d_ref[j] * (length - 1 - iota((length, LANES), 0)).astype(f32)))
-        gr_own[pl.ds(j, 1)] = jnp.sum(jnp.where(pick, full, 0.0), axis=0, keepdims=True).reshape(1, 1, LANES)
+        full = mm3(lags[...], jnp.exp(-d_row[j] * (length - 1 - iota((length, LANES), 0)).astype(f32)))
+        own_row[j] = jnp.sum(jnp.where(pick, full, 0.0), axis=0, keepdims=True)
 
     steps = max(nb, nc + nz)
 
@@ -211,24 +237,19 @@
 
     lax.fori_loop(0, steps, second, 0)
 
-    def carries(j, c):
+    def carries(j, acc):
         f = fade(j)
         zf, zb = zf_in[j], zb_in[j]
         cf = jnp.where(side == 0, zf, f * zf + peer[j, 0])
         cb = jnp.where(side == 0, f * zb + peer[j, 1], zb)
         zf_in[j] = cf
         zb_in[j] = cb
-        hi, lo = split(own[j, 1] * cf)
-        cross = mm(hi, pick16, 1, 1) + mm(lo, pick16, 1, 1)
-        gr_own[nb + j] = fold(cross)
-        return c
-
-    def fold(cross):
-        spread = mm3(cross, jnp.where(pick, 1.0, 0.0))
-        keep = lax.rem(iota((ORDER, ROWS), 1), ORDER) == iota((ORDER, ROWS), 0)
-        return jnp.sum(jnp.where(keep, spread, 0.0), axis=0, keepdims=True)
-
-    lax.fori_loop(0, nb, carries, 0)
+        own_mode = lax.rem(iota((ORDER, LANES), 1), ORDER) == iota((ORDER, LANES), 0)
+        hi, lo = split(own[j, 1] * cf + jnp.where(own_mode, own_row[j], 0.0))
+        hot = chosen(j)
+        return acc + mm(hi, hot, 1, 1) + mm(lo, hot, 1, 1)
+
+    gr_own[...] = lax.fori_loop(0, nb, carries, jnp.zeros(gr_own.shape, f32))
 
     def gcopy(i):
         to = lax.rem(me + i, n)
@@ -244,15 +265,15 @@
 
     def last(j, c):
         cols = pl.ds(pl.multiple_of(j * LANES, LANES), LANES)
-        r = r_ref[j]
+        r = r_row[j]
         cf = jnp.where(diag, jnp.concatenate([zf_in[j]] * PER, 0), 0.0)
         cb = jnp.where(diag, jnp.concatenate([zb_in[j]] * PER, 0), 0.0)
         m = mix[:, cols] + mm3(r * w0[:, cols], cf)
         gsv = gsig[:, cols] + mm3(r * w1[:, cols], cb)
-        out_ref[:, cols] = (q_ref[:, cols].astype(f32) * m).astype(bf16)
-        dq_ref[:, cols] = (g_ref[:, cols].astype(f32) * m).astype(bf16)
-        dk_ref[:, cols] = (gsv * v_ref[:, cols].astype(f32)).astype(bf16)
-        dv_ref[:, cols] = (gsv * k_ref[:, cols].astype(f32)).astype(bf16)
+        out_ref[:, cols] = (x_ref[0, :, cols].astype(f32) * m).astype(bf16)
+        dx_ref[0, :, cols] = (g_ref[:, cols].astype(f32) * m).astype(bf16)
+        dx_ref[1, :, cols] = (gsv * x_ref[2, :, cols].astype(f32)).astype(bf16)
+        dx_ref[2, :, cols] = (gsv * x_ref[1, :, cols].astype(f32)).astype(bf16)
         return c
 
     lax.fori_loop(0, nb, last, 0)
@@ -289,18 +310,18 @@
     nb = channels // LANES
     per_chunk = 2
     nc = nb // per_chunk
-    q, k, v = qkv[:, 0], qkv[:, 1], qkv[:, 2]
-    d_row = decay.reshape(nb, 1, ROWS)
-    r_row = residue.reshape(nb, 1, ROWS)
-    drep = jnp.repeat(decay.T, GROUP, axis=1)
     wide = jax.ShapeDtypeStruct((length, channels), bf16)
     vm = pl.BlockSpec(memory_space=pltpu.VMEM)
     dma = pltpu.SemaphoreType.DMA
-    out, dq, dk, dv, gr = pl.pallas_call(
+    out, dx, gr = pl.pallas_call(
         functools.partial(kernel, n, nb, per_chunk, length),
-        out_shape=(wide, wide, wide, wide, jax.ShapeDtypeStruct((2 * nb, 1, ROWS), f32)),
-        in_specs=[vm] * 7,
-        out_specs=(vm,) * 5,
+        out_shape=(
+            wide,
+            jax.ShapeDtypeStruct((3, length, channels), bf16),
+            jax.ShapeDtypeStruct((ORDER, nb * PER), f32),
+        ),
+        in_specs=[vm] * 4,
+        out_specs=(vm,) * 3,
         scratch_shapes=[
             pltpu.VMEM((length, channels), bf16),
             pltpu.VMEM((length, channels), bf16),
@@ -315,16 +336,20 @@
             pltpu.VMEM((nb, ORDER, LANES), f32),
             pltpu.VMEM((nb, ORDER, LANES), f32),
             pltpu.VMEM((PER, length), f32),
-            pltpu.VMEM((2 * nb, 1, ROWS), f32),
-            pltpu.VMEM((n, 2 * nb, 1, ROWS), f32),
+            pltpu.VMEM((ORDER, nb * PER), f32),
+            pltpu.VMEM((n, ORDER, nb * PER), f32),
+            pltpu.VMEM((nb, ORDER, LANES), f32),
+            pltpu.VMEM((nb, 1, LANES), f32),
+            pltpu.VMEM((nb, 1, LANES), f32),
+            pltpu.VMEM((nb, 1, LANES), f32),
+            pltpu.VMEM((3, 8 * length, 128), bf16),
             dma((nc,)), dma((nc,)), dma((nc,)), dma((nc,)), dma((nc,)), dma((nc,)),
             dma((n,)), dma((n,)),
         ],
         compiler_params=pltpu.CompilerParams(
             collective_id=0, has_side_effects=True, vmem_limit_bytes=56 * 1024 * 1024),
-    )(q, k, v, g_out, d_row, r_row, drep)
-    grad_res = (gr[:nb] + gr[nb:]).reshape(nb * PER, ORDER)
-    return out, jnp.stack([dq, dk, dv], 1), grad_res
+    )(jnp.transpose(qkv, (1, 0, 2)), g_out, decay.T, residue.T)
+    return out, jnp.transpose(dx, (1, 0, 2)), gr.T
 
 
 def solution(mesh):

time: 77.3 us -> 69 us (0.89)
  local copies, waits for them, and re-layouts: 12 us -> 6.82 us
  other arithmetic: 3.99 us -> 0 us
  Pallas kernels: 60.2 us -> 61.3 us
    another operation x1 -> x0, other arithmetic: 3.95 us -> none  [on_device(): return (out, jnp.stack([dq, dk, dv], 1), grad_res)]
    reshape x4 -> x0, local copies, waits for them, and re-layouts: 3.79 us -> none  [the longest x1 2.27 us: on_device(): drep = jnp.repeat(decay.T, GROUP, axis=1)]
    squeeze x1 -> x0, local copies, waits for them, and re-layouts: 3.62 us -> none  [on_device(): q, k, v = (qkv[:, 0], qkv[:, 1], qkv[:, 2])]
    unnamed x8 -> x5, local copies, waits for them, and re-layouts: 3.29 us -> 6.82 us
    broadcast_in_dim x1 -> x0, local copies, waits for them, and re-layouts: 1.31 us -> none  [on_device(): drep = jnp.repeat(decay.T, GROUP, axis=1)]
    pallas_call x1, Pallas kernels: 60.2 us -> 61.3 us  [on_device(): pl.pallas_call(functools.partial(kernel, n, nb, per_chunk, length), out_s...]
where the time goes in v1:
time: 69 us; the launch traced here: 68.8 us
  Pallas kernels  61.3 us (89%)
  local copies, waits for them, and re-layouts  6.82 us (10%)
    pallas_call x1, Pallas kernels, on_device(): pl.pallas_call(functools.partial(kernel, n, nb, per_chunk, length), out_s...  61.3 us
    unnamed x5, local copies, waits for them, and re-layouts  6.82 us

profile of v1, /device:TPU:0, one launch (start us, length us, event | category | flops | bytes accessed | tf_op | source)
XLA Modules:
  0.0 68.8 jit_solution(6770103898132136328)
XLA Ops:
  0.6 61.3 %shard_map.67 = (bf16[128,4096]{1,0:T(8,128)(2,1)}, bf16[3,128,4096]{2,1,0:T(8,128)(2,1)}, f32[16,256]{1,0:T(8,128)}) custom-call(bf16[3,128,4096]{2,1,0:T(8,128)(2,1)} %bitcast.6, bf16[128,4096]{1,0:T(8,128)(2,1)} %g_ref.1, f32[16,256]{1,0:T(8,128)} %bitcast.7, f32[16,256]{1,0:T(8,128)} %bitcast.8), custom_call_target="tpu_custom_call" | custom-call | tf_op jit(solution)/shard_map/pallas_call | solution.py:316
  62.0 2.3 %copy.10 = bf16[128,4096]{1,0:T(8,128)(2,1)} copy(bf16[128,4096]{1,0:T(8,128)(2,1)} %get-tuple-element.12) | data formatting | bytes 2097152
  64.3 0.0 copy-start
  64.3 3.9 %copy.11 = bf16[128,3,4096]{2,0,1:T(8,128)(2,1)} copy(bf16[128,3,4096]{2,0,1:T(8,128)(2,1)} %bitcast.5) | data formatting | bytes 6291456
  68.2 0.0 copy-done
  68.2 0.6 copy.12
Async XLA Ops:
  64.3 3.9 %copy-start = (f32[16,256]{1,0:T(8,128)S(1)}, f32[16,256]{1,0:T(8,128)}, u32[]{:S(2)}) copy-start(f32[16,256]{1,0:T(8,128)} %get-tuple-element.8) | copy-start | bytes 49156

commit v2 on v1

--- a/solution.py
+++ b/solution.py
@@ -14,6 +14,8 @@
 bf16 = jnp.bfloat16
 f32 = jnp.float32
 PAIR = 2
+LEAD = 1
+SLACK = 2
 
 
 def split(a):
@@ -116,8 +118,20 @@
         xcopy(i).start()
         return c
 
+    early = (3 * nc) // 4
+
+    def ahead(j, c):
+        states(j, 0)
+        return c
+
+    def send(i, c):
+        xcopy(i).start()
+        return c
+
+    lax.fori_loop(0, early * per_chunk, ahead, 0)
     pl.semaphore_wait(barrier, n - 1)
-    lax.fori_loop(0, nc, first, 0)
+    lax.fori_loop(0, early, send, 0)
+    lax.fori_loop(early, nc, first, 0)
 
     def fade(j):
         return drep[j]
@@ -173,10 +187,10 @@
         full = mm3(lags[...], jnp.exp(-d_row[j] * (length - 1 - iota((length, LANES), 0)).astype(f32)))
         own_row[j] = jnp.sum(jnp.where(pick, full, 0.0), axis=0, keepdims=True)
 
-    steps = max(nb, nc + nz)
+    steps = max(nb, LEAD + nc + SLACK * (nz - 1))
 
     def comm(step):
-        i = step - z
+        i = step - SLACK * z
 
         @pl.when((i >= 0) & (i < nc))
         def _():
@@ -194,7 +208,7 @@
                     zf_out[j] = pair + jnp.where(z > 0, f * f * zf_in[j], 0.0)
                 zcopy(i, True).start()
 
-        i2 = step - (nz - 1 - z)
+        i2 = step - SLACK * (nz - 1 - z)
 
         @pl.when((i2 >= 0) & (i2 < nc))
         def _():
@@ -225,13 +239,13 @@
         def _():
             heavy(s)
 
-        @pl.when((s >= 1) & (s - 1 < nc))
-        def _():
-            xcopy(s - 1).wait_recv()
-
-        @pl.when(s >= 1)
-        def _():
-            comm(s - 1)
+        @pl.when((s >= LEAD) & (s - LEAD < nc))
+        def _():
+            xcopy(s - LEAD).wait_recv()
+
+        @pl.when(s >= LEAD)
+        def _():
+            comm(s - LEAD)
 
         return c
 
@@ -303,6 +317,30 @@
         return acc + gr_all[i]
 
     gr_ref[...] = lax.fori_loop(1, n, gsum, gr_own[...])
+
+
+def pass_on(a_ref, b_ref, c_ref, x_ref, y_ref, z_ref):
+    x_ref[...] = a_ref[...]
+    y_ref[...] = b_ref[...]
+    z_ref[...] = c_ref[...]
+
+
+def settle(out, dx, gr):
+    length, channels = out.shape
+    width = min(1024, channels)
+    specs = (
+        pl.BlockSpec((length, width), lambda i: (0, i)),
+        pl.BlockSpec((3, length, width), lambda i: (0, 0, i)),
+        pl.BlockSpec(gr.shape, lambda i: (0, 0)),
+    )
+    return pl.pallas_call(
+        pass_on,
+        grid=(channels // width,),
+        out_shape=tuple(jax.ShapeDtypeStruct(a.shape, a.dtype) for a in (out, dx, gr)),
+        in_specs=list(specs),
+        out_specs=specs,
+        compiler_params=pltpu.CompilerParams(vmem_limit_bytes=16 * 1024 * 1024),
+    )(out, dx, gr)
 
 
 def on_device(n, qkv, g_out, residue, decay):
@@ -347,8 +385,9 @@
             dma((n,)), dma((n,)),
         ],
         compiler_params=pltpu.CompilerParams(
-            collective_id=0, has_side_effects=True, vmem_limit_bytes=56 * 1024 * 1024),
+            collective_id=0, has_side_effects=True, vmem_limit_bytes=40 * 1024 * 1024),
     )(jnp.transpose(qkv, (1, 0, 2)), g_out, decay.T, residue.T)
+    out, dx, gr = settle(out, dx, gr)
     return out, jnp.transpose(dx, (1, 0, 2)), gr.T
 
 

time: 69 us -> 51.9 us (0.75)
  Pallas kernels: 61.3 us -> 46.4 us
  local copies, waits for them, and re-layouts: 6.82 us -> 4.54 us
    pallas_call x1, Pallas kernels: 61.3 us -> 43.8 us  [on_device(): pl.pallas_call(functools.partial(kernel, n, nb, per_chunk, length), out_s...]
    pallas_call x0 -> x1, Pallas kernels: none -> 2.68 us  [settle(): pl.pallas_call(pass_on, grid=(channels // width,), out_shape=tuple((jax.S...]
    unnamed x5 -> x8, local copies, waits for them, and re-layouts: 6.82 us -> 4.54 us
where the time goes in v2:
time: 51.9 us; the launch traced here: 51.6 us
  Pallas kernels  46.4 us (89%)
  local copies, waits for them, and re-layouts  4.54 us (9%)
  between operations  0.65 us (1%)
    pallas_call x1, Pallas kernels, on_device(): pl.pallas_call(functools.partial(kernel, n, nb, per_chunk, length), out_s...  43.8 us
    unnamed x8, local copies, waits for them, and re-layouts  4.54 us
    pallas_call x1, Pallas kernels, settle(): pl.pallas_call(pass_on, grid=(channels // width,), out_shape=tuple((jax.S...  2.68 us

profile of v2, /device:TPU:0, one launch (start us, length us, event | category | flops | bytes accessed | tf_op | source)
XLA Modules:
  0.0 51.6 jit_solution(5981751369872810694)
XLA Ops:
  0.6 0.0 copy-start
  0.6 1.9 %copy-done = bf16[128,3,4096]{2,0,1:T(8,128)(2,1)S(1)} copy-done((bf16[128,3,4096]{2,0,1:T(8,128)(2,1)S(1)}, bf16[128,3,4096]{2,0,1:T(8,128)(2,1)}, u32[]{:S(2)}) %copy-start) | copy-done | bytes 3145752
  2.5 0.0 copy-start.1
  2.5 1.2 %copy-done.1 = bf16[128,4096]{1,0:T(8,128)(2,1)S(1)} copy-done((bf16[128,4096]{1,0:T(8,128)(2,1)S(1)}, bf16[128,4096]{1,0:T(8,128)(2,1)}, u32[]{:S(2)}) %copy-start.1) | copy-done | bytes 1048600
  3.7 0.0 copy-start.2
  3.7 0.7 %copy-done.2 = f32[256,16]{0,1:T(8,128)S(1)} copy-done((f32[256,16]{0,1:T(8,128)S(1)}, f32[256,16]{0,1:T(8,128)}, u32[]{:S(2)}) %copy-start.2) | copy-done | bytes 16408
  4.5 0.0 copy-start.3
  4.5 0.7 %copy-done.3 = f32[256,16]{0,1:T(8,128)S(1)} copy-done((f32[256,16]{0,1:T(8,128)S(1)}, f32[256,16]{0,1:T(8,128)}, u32[]{:S(2)}) %copy-start.3) | copy-done | bytes 16408
  5.2 43.8 %shard_map.67 = (bf16[128,4096]{1,0:T(8,128)(2,1)S(1)}, bf16[3,128,4096]{2,1,0:T(8,128)(2,1)S(1)}, f32[16,256]{1,0:T(8,128)S(1)}) custom-call(bf16[3,128,4096]{2,1,0:T(8,128)(2,1)S(1)} %bitcast.5, bf16[128,4096]{1,0:T(8,128)(2,1)S(1)} %copy-done.1, f32[16,256]{1,0:T(8,128)S(1)} %bitcast.6, f32[16,256]{1,0:T(8,128)S(1)} %bitcast.7), custom_call_target="tpu_custom_call" | custom-call | tf_op jit(solution)/shard_map/pallas_call | solution.py:354
  48.9 2.7 %shard_map.68 = (bf16[128,4096]{1,0:T(8,128)(2,1)}, bf16[3,128,4096]{2,1,0:T(8,128)(2,1)}, f32[16,256]{1,0:T(8,128)}) custom-call(bf16[128,4096]{1,0:T(8,128)(2,1)S(1)} %get-tuple-element.9.a_ref, bf16[3,128,4096]{2,1,0:T(8,128)(2,1)S(1)} %get-tuple-element.10.b_ref, f32[16,256]{1,0:T(8,128)S(1)} %get-tuple-element.11.c_ref), custom_call_target="tpu_custom_call" | custom-call | tf_op jit(solution)/shard_map/pallas_call | solution.py:336
Async XLA Ops:
  0.6 1.9 %copy-start = (bf16[128,3,4096]{2,0,1:T(8,128)(2,1)S(1)}, bf16[128,3,4096]{2,0,1:T(8,128)(2,1)}, u32[]{:S(2)}) copy-start(bf16[128,3,4096]{2,0,1:T(8,128)(2,1)} %param.4) | copy-start | bytes 9437188
  2.5 1.2 %copy-start.1 = (bf16[128,4096]{1,0:T(8,128)(2,1)S(1)}, bf16[128,4096]{1,0:T(8,128)(2,1)}, u32[]{:S(2)}) copy-start(bf16[128,4096]{1,0:T(8,128)(2,1)} %g_ref.1) | copy-start | bytes 3145732
  3.7 0.7 %copy-start.2 = (f32[256,16]{0,1:T(8,128)S(1)}, f32[256,16]{0,1:T(8,128)}, u32[]{:S(2)}) copy-start(f32[256,16]{0,1:T(8,128)} %param.7) | copy-start | bytes 49156
  4.5 0.7 %copy-start.3 = (f32[256,16]{0,1:T(8,128)S(1)}, f32[256,16]{0,1:T(8,128)}, u32[]{:S(2)}) copy-start(f32[256,16]{0,1:T(8,128)} %param.6) | copy-start | bytes 49156

commit v3 on v2

--- a/solution.py
+++ b/solution.py
@@ -15,7 +15,7 @@
 f32 = jnp.float32
 PAIR = 2
 LEAD = 1
-SLACK = 2
+SLACK = 3
 
 
 def split(a):
@@ -39,10 +39,10 @@
 
 def kernel(
     n, nb, per_chunk, length,
-    x_ref, g_ref, dt_ref, rt_ref,
+    x_hbm, g_hbm, dt_ref, rt_ref,
     out_ref, dx_ref, gr_ref,
-    sig, cot, w0, w1, mix, gsig, own, peer, zf_in, zf_out, zb_in, zb_out, lags, gr_own, gr_all, drep, d_row, r_row, own_row, tmat,
-    xs, xr, fs, fr, bs, br, gs, grs,
+    sig, cot, w0, w1, mix, gsig, own, peer, zf_in, zf_out, zb_in, zb_out, lags, gr_own, gr_all, drep, d_row, r_row, own_row, tmat, pmat, x_ref, g_ref,
+    xs, xr, fs, fr, bs, br, gs, grs, xin, gin,
 ):
     me = lax.axis_index("ctx")
     side = lax.rem(me, PAIR)
@@ -52,6 +52,19 @@
     partner = me + 1 - 2 * side
     half = 128
 
+    def load(i):
+        cols = pl.ds(pl.multiple_of(i * per_chunk * LANES, LANES), per_chunk * LANES)
+        return (
+            pltpu.make_async_copy(x_hbm.at[:, :, cols], x_ref.at[:, :, cols], xin.at[i]),
+            pltpu.make_async_copy(g_hbm.at[:, cols], g_ref.at[:, cols], gin.at[i]),
+        )
+
+    def load_start(i, c):
+        for copy in load(i):
+            copy.start()
+        return c
+
+    lax.fori_loop(0, nc, load_start, 0)
     barrier = pltpu.get_barrier_semaphore()
 
     def greet(i, c):
@@ -113,22 +126,24 @@
             device_id={"ctx": to}, device_id_type=pl.DeviceIdType.MESH)
 
     def first(i, c):
+        ahead(i, 0)
+        xcopy(i).start()
+        return c
+
+    def ahead(i, c):
+        for copy in load(i):
+            copy.wait()
         for u in range(per_chunk):
             states(i * per_chunk + u, 0)
-        xcopy(i).start()
         return c
 
     early = (3 * nc) // 4
-
-    def ahead(j, c):
-        states(j, 0)
-        return c
 
     def send(i, c):
         xcopy(i).start()
         return c
 
-    lax.fori_loop(0, early * per_chunk, ahead, 0)
+    lax.fori_loop(0, early, ahead, 0)
     pl.semaphore_wait(barrier, n - 1)
     lax.fori_loop(0, early, send, 0)
     lax.fori_loop(early, nc, first, 0)
@@ -154,33 +169,41 @@
         h1, l1 = split(r * jnp.where(row0, 1.0, a1))
         h = mm(pick16, h0, 1, 1) + mm(pick16, l0, 1, 1)
         hr = mm(pick16, h1, 1, 1) + mm(pick16, l1, 1, 1)
+        blank = jnp.zeros((length, half), bf16)
+
+        def corners(a, b):
+            return jnp.concatenate(
+                [jnp.concatenate([a, blank], 1), jnp.concatenate([blank, b], 1)], 0)
+
+        sgw = sig[:, cols]
+        ctw = cot[:, cols]
+        back = mm(flip, ctw).astype(bf16)
+        per_half = half // GROUP
+        lane_group = iota((length, half), 1) // GROUP
+        for e in range(per_half):
+            keep = lax.rem(iota((1, LANES), 1) // GROUP, per_half) == e
+            pmat[pl.ds(e * length, length)] = back * jnp.where(keep, 1.0, 0.0).astype(bf16)
+        pall = mm(pmat[...], corners(sgw[:, :half], sgw[:, half:]), 1, 1)
         for p in range(LANES // half):
             hc = pl.ds(pl.multiple_of(j * LANES + p * half, half), half)
-            sg = sig[:, hc]
-            ct = cot[:, hc]
-            back = mm(flip, ct)
-            lane_group = iota((length, half), 1) // GROUP
-            back16 = back.astype(bf16)
-            for e in range(half // GROUP):
-                g = p * (half // GROUP) + e
+            side_cols = slice(p * half, (p + 1) * half)
+            for e in range(per_half):
+                g = p * per_half + e
                 rows = pl.ds(e * length, length)
                 tt = pltpu.roll(jnp.broadcast_to(h[g:g + 1], (length, length)), 0, 1, stride=1, stride_axis=0)
-                tmat[0, rows] = jnp.where(upper, tt, 0.0).astype(bf16)
+                tmat[p, rows, half:] = jnp.where(upper, tt, 0.0).astype(bf16)
                 tf = pltpu.roll(jnp.broadcast_to(hr[g:g + 1], (length, length)), 0, 1, stride=1, stride_axis=0)
-                tmat[1, rows] = jnp.where(lower, tf, 0.0).astype(bf16)
-                tmat[2, rows] = back16 * jnp.where(iota((1, half), 1) // GROUP == e, 1.0, 0.0).astype(bf16)
-            gall = mm(tmat[0], ct)
-            mall = mm(tmat[1], sg)
-            pall = mm(tmat[2], sg, 1, 1)
-            gacc = gall[:length]
-            macc = mall[:length]
-            for e in range(half // GROUP):
-                g = p * (half // GROUP) + e
+                tmat[p, rows, :half] = jnp.where(lower, tf, 0.0).astype(bf16)
+            both = mm(tmat[p], corners(sgw[:, side_cols], ctw[:, side_cols]))
+            macc = both[:length, :half]
+            gacc = both[:length, half:]
+            for e in range(per_half):
+                g = p * per_half + e
                 at = slice(e * length, (e + 1) * length)
                 if e:
-                    gacc = jnp.where(lane_group == e, gall[at], gacc)
-                    macc = jnp.where(lane_group == e, mall[at], macc)
-                m = pltpu.roll(jnp.where(corner, pall[at], 0.0), 0, 1, stride=1, stride_axis=0)
+                    macc = jnp.where(lane_group == e, both[at, :half], macc)
+                    gacc = jnp.where(lane_group == e, both[at, half:], gacc)
+                m = pltpu.roll(jnp.where(corner, pall[at, side_cols], 0.0), 0, 1, stride=1, stride_axis=0)
                 lags[g:g + 1, :] = jnp.sum(m, axis=0, keepdims=True)
             mix[:, hc] = macc
             gsig[:, hc] = gacc
@@ -263,7 +286,7 @@
         hot = chosen(j)
         return acc + mm(hi, hot, 1, 1) + mm(lo, hot, 1, 1)
 
-    gr_own[...] = lax.fori_loop(0, nb, carries, jnp.zeros(gr_own.shape, f32))
+    gr_own[...] = lax.fori_loop(0, nb, carries, jnp.zeros(gr_own.shape, f32), unroll=4)
 
     def gcopy(i):
         to = lax.rem(me + i, n)
@@ -290,7 +313,7 @@
         dx_ref[2, :, cols] = (gsv * x_ref[1, :, cols].astype(f32)).astype(bf16)
         return c
 
-    lax.fori_loop(0, nb, last, 0)
+    lax.fori_loop(0, nb, last, 0, unroll=2)
 
     def xend(i, c):
         xcopy(i).wait_send()
@@ -358,7 +381,7 @@
             jax.ShapeDtypeStruct((3, length, channels), bf16),
             jax.ShapeDtypeStruct((ORDER, nb * PER), f32),
         ),
-        in_specs=[vm] * 4,
+        in_specs=[pl.BlockSpec(memory_space=pltpu.HBM)] * 2 + [vm] * 2,
         out_specs=(vm,) * 3,
         scratch_shapes=[
             pltpu.VMEM((length, channels), bf16),
@@ -380,9 +403,12 @@
             pltpu.VMEM((nb, 1, LANES), f32),
             pltpu.VMEM((nb, 1, LANES), f32),
             pltpu.VMEM((nb, 1, LANES), f32),
-            pltpu.VMEM((3, 8 * length, 128), bf16),
+            pltpu.VMEM((2, 8 * length, LANES), bf16),
+            pltpu.VMEM((8 * length, LANES), bf16),
+            pltpu.VMEM((3, length, channels), bf16),
+            pltpu.VMEM((length, channels), bf16),
             dma((nc,)), dma((nc,)), dma((nc,)), dma((nc,)), dma((nc,)), dma((nc,)),
-            dma((n,)), dma((n,)),
+            dma((n,)), dma((n,)), dma((nc,)), dma((nc,)),
         ],
         compiler_params=pltpu.CompilerParams(
             collective_id=0, has_side_effects=True, vmem_limit_bytes=40 * 1024 * 1024),

time: 51.9 us -> 46.8 us (0.902)
  Pallas kernels: 46.4 us -> 41.3 us
    pallas_call x1, Pallas kernels: 43.8 us -> 38.6 us  [on_device(): pl.pallas_call(functools.partial(kernel, n, nb, per_chunk, length), out_s...]
where the time goes in v3:
time: 46.8 us; the launch traced here: 46.5 us
  Pallas kernels  41.3 us (88%)
  local copies, waits for them, and re-layouts  4.54 us (10%)
  between operations  0.65 us (1%)
    pallas_call x1, Pallas kernels, on_device(): pl.pallas_call(functools.partial(kernel, n, nb, per_chunk, length), out_s...  38.6 us
    unnamed x8, local copies, waits for them, and re-layouts  4.54 us
    pallas_call x1, Pallas kernels, settle(): pl.pallas_call(pass_on, grid=(channels // width,), out_shape=tuple((jax.S...  2.68 us

profile of v3, /device:TPU:0, one launch (start us, length us, event | category | flops | bytes accessed | tf_op | source)
XLA Modules:
  0.0 46.5 jit_solution(7225188515981479546)
XLA Ops:
  0.6 0.0 copy-start
  0.6 1.9 %copy-done = bf16[128,3,4096]{2,0,1:T(8,128)(2,1)S(1)} copy-done((bf16[128,3,4096]{2,0,1:T(8,128)(2,1)S(1)}, bf16[128,3,4096]{2,0,1:T(8,128)(2,1)}, u32[]{:S(2)}) %copy-start) | copy-done | bytes 3145752
  2.5 0.0 copy-start.1
  2.5 1.2 %copy-done.1 = bf16[128,4096]{1,0:T(8,128)(2,1)S(1)} copy-done((bf16[128,4096]{1,0:T(8,128)(2,1)S(1)}, bf16[128,4096]{1,0:T(8,128)(2,1)}, u32[]{:S(2)}) %copy-start.1) | copy-done | bytes 1048600
  3.7 0.0 copy-start.2
  3.7 0.7 %copy-done.2 = f32[256,16]{0,1:T(8,128)S(1)} copy-done((f32[256,16]{0,1:T(8,128)S(1)}, f32[256,16]{0,1:T(8,128)}, u32[]{:S(2)}) %copy-start.2) | copy-done | bytes 16408
  4.5 0.0 copy-start.3
  4.5 0.7 %copy-done.3 = f32[256,16]{0,1:T(8,128)S(1)} copy-done((f32[256,16]{0,1:T(8,128)S(1)}, f32[256,16]{0,1:T(8,128)}, u32[]{:S(2)}) %copy-start.3) | copy-done | bytes 16408
  5.2 38.6 %shard_map.67 = (bf16[128,4096]{1,0:T(8,128)(2,1)S(1)}, bf16[3,128,4096]{2,1,0:T(8,128)(2,1)S(1)}, f32[16,256]{1,0:T(8,128)S(1)}) custom-call(bf16[3,128,4096]{2,1,0:T(8,128)(2,1)S(1)} %bitcast.5, bf16[128,4096]{1,0:T(8,128)(2,1)S(1)} %copy-done.1, f32[16,256]{1,0:T(8,128)S(1)} %bitcast.6, f32[16,256]{1,0:T(8,128)S(1)} %bitcast.7), custom_call_target="tpu_custom_call" | custom-call | tf_op jit(solution)/shard_map/pallas_call | solution.py:377
  43.8 2.7 %shard_map.68 = (bf16[128,4096]{1,0:T(8,128)(2,1)}, bf16[3,128,4096]{2,1,0:T(8,128)(2,1)}, f32[16,256]{1,0:T(8,128)}) custom-call(bf16[128,4096]{1,0:T(8,128)(2,1)S(1)} %get-tuple-element.9.a_ref, bf16[3,128,4096]{2,1,0:T(8,128)(2,1)S(1)} %get-tuple-element.10.b_ref, f32[16,256]{1,0:T(8,128)S(1)} %get-tuple-element.11.c_ref), custom_call_target="tpu_custom_call" | custom-call | tf_op jit(solution)/shard_map/pallas_call | solution.py:359
Async XLA Ops:
  0.6 1.9 %copy-start = (bf16[128,3,4096]{2,0,1:T(8,128)(2,1)S(1)}, bf16[128,3,4096]{2,0,1:T(8,128)(2,1)}, u32[]{:S(2)}) copy-start(bf16[128,3,4096]{2,0,1:T(8,128)(2,1)} %param.4) | copy-start | bytes 9437188
  2.5 1.2 %copy-start.1 = (bf16[128,4096]{1,0:T(8,128)(2,1)S(1)}, bf16[128,4096]{1,0:T(8,128)(2,1)}, u32[]{:S(2)}) copy-start(bf16[128,4096]{1,0:T(8,128)(2,1)} %g_hbm.1) | copy-start | bytes 3145732
  3.7 0.7 %copy-start.2 = (f32[256,16]{0,1:T(8,128)S(1)}, f32[256,16]{0,1:T(8,128)}, u32[]{:S(2)}) copy-start(f32[256,16]{0,1:T(8,128)} %param.7) | copy-start | bytes 49156
  4.5 0.7 %copy-start.3 = (f32[256,16]{0,1:T(8,128)S(1)}, f32[256,16]{0,1:T(8,128)}, u32[]{:S(2)}) copy-start(f32[256,16]{0,1:T(8,128)} %param.6) | copy-start | bytes 49156

commit v4 on v3

--- a/solution.py
+++ b/solution.py
@@ -137,7 +137,7 @@
             states(i * per_chunk + u, 0)
         return c
 
-    early = (3 * nc) // 4
+    early = nc // 2
 
     def send(i, c):
         xcopy(i).start()
@@ -350,7 +350,7 @@
 
 def settle(out, dx, gr):
     length, channels = out.shape
-    width = min(1024, channels)
+    width = min(2048, channels)
     specs = (
         pl.BlockSpec((length, width), lambda i: (0, i)),
         pl.BlockSpec((3, length, width), lambda i: (0, 0, i)),

time: 46.8 us -> 45.5 us (0.972)
  Pallas kernels: 41.3 us -> 40 us
    pallas_call x1, Pallas kernels: 38.6 us -> 37.5 us  [on_device(): pl.pallas_call(functools.partial(kernel, n, nb, per_chunk, length), out_s...]
where the time goes in v4:
time: 45.5 us; the launch traced here: 45.1 us
  Pallas kernels  40 us (88%)
  local copies, waits for them, and re-layouts  4.54 us (10%)
  between operations  0.65 us (1%)
    pallas_call x1, Pallas kernels, on_device(): pl.pallas_call(functools.partial(kernel, n, nb, per_chunk, length), out_s...  37.5 us
    unnamed x8, local copies, waits for them, and re-layouts  4.54 us
    pallas_call x1, Pallas kernels, settle(): pl.pallas_call(pass_on, grid=(channels // width,), out_shape=tuple((jax.S...  2.47 us

profile of v4, /device:TPU:0, one launch (start us, length us, event | category | flops | bytes accessed | tf_op | source)
XLA Modules:
  0.0 45.1 jit_solution(4376465150780597830)
XLA Ops:
  0.6 0.0 copy-start
  0.6 1.9 %copy-done = bf16[128,3,4096]{2,0,1:T(8,128)(2,1)S(1)} copy-done((bf16[128,3,4096]{2,0,1:T(8,128)(2,1)S(1)}, bf16[128,3,4096]{2,0,1:T(8,128)(2,1)}, u32[]{:S(2)}) %copy-start) | copy-done | bytes 3145752
  2.5 0.0 copy-start.1
  2.5 1.2 %copy-done.1 = bf16[128,4096]{1,0:T(8,128)(2,1)S(1)} copy-done((bf16[128,4096]{1,0:T(8,128)(2,1)S(1)}, bf16[128,4096]{1,0:T(8,128)(2,1)}, u32[]{:S(2)}) %copy-start.1) | copy-done | bytes 1048600
  3.7 0.0 copy-start.2
  3.7 0.7 %copy-done.2 = f32[256,16]{0,1:T(8,128)S(1)} copy-done((f32[256,16]{0,1:T(8,128)S(1)}, f32[256,16]{0,1:T(8,128)}, u32[]{:S(2)}) %copy-start.2) | copy-done | bytes 16408
  4.5 0.0 copy-start.3
  4.5 0.7 %copy-done.3 = f32[256,16]{0,1:T(8,128)S(1)} copy-done((f32[256,16]{0,1:T(8,128)S(1)}, f32[256,16]{0,1:T(8,128)}, u32[]{:S(2)}) %copy-start.3) | copy-done | bytes 16408
  5.2 37.5 %shard_map.67 = (bf16[128,4096]{1,0:T(8,128)(2,1)S(1)}, bf16[3,128,4096]{2,1,0:T(8,128)(2,1)S(1)}, f32[16,256]{1,0:T(8,128)S(1)}) custom-call(bf16[3,128,4096]{2,1,0:T(8,128)(2,1)S(1)} %bitcast.5, bf16[128,4096]{1,0:T(8,128)(2,1)S(1)} %copy-done.1, f32[16,256]{1,0:T(8,128)S(1)} %bitcast.6, f32[16,256]{1,0:T(8,128)S(1)} %bitcast.7), custom_call_target="tpu_custom_call" | custom-call | tf_op jit(solution)/shard_map/pallas_call | solution.py:377
  42.7 2.5 %shard_map.68 = (bf16[128,4096]{1,0:T(8,128)(2,1)}, bf16[3,128,4096]{2,1,0:T(8,128)(2,1)}, f32[16,256]{1,0:T(8,128)}) custom-call(bf16[128,4096]{1,0:T(8,128)(2,1)S(1)} %get-tuple-element.9.a_ref, bf16[3,128,4096]{2,1,0:T(8,128)(2,1)S(1)} %get-tuple-element.10.b_ref, f32[16,256]{1,0:T(8,128)S(1)} %get-tuple-element.11.c_ref), custom_call_target="tpu_custom_call" | custom-call | tf_op jit(solution)/shard_map/pallas_call | solution.py:359
Async XLA Ops:
  0.6 1.9 %copy-start = (bf16[128,3,4096]{2,0,1:T(8,128)(2,1)S(1)}, bf16[128,3,4096]{2,0,1:T(8,128)(2,1)}, u32[]{:S(2)}) copy-start(bf16[128,3,4096]{2,0,1:T(8,128)(2,1)} %param.4) | copy-start | bytes 9437188
  2.5 1.2 %copy-start.1 = (bf16[128,4096]{1,0:T(8,128)(2,1)S(1)}, bf16[128,4096]{1,0:T(8,128)(2,1)}, u32[]{:S(2)}) copy-start(bf16[128,4096]{1,0:T(8,128)(2,1)} %g_hbm.1) | copy-start | bytes 3145732
  3.7 0.7 %copy-start.2 = (f32[256,16]{0,1:T(8,128)S(1)}, f32[256,16]{0,1:T(8,128)}, u32[]{:S(2)}) copy-start(f32[256,16]{0,1:T(8,128)} %param.7) | copy-start | bytes 49156
  4.5 0.7 %copy-start.3 = (f32[256,16]{0,1:T(8,128)S(1)}, f32[256,16]{0,1:T(8,128)}, u32[]{:S(2)}) copy-start(f32[256,16]{0,1:T(8,128)} %param.6) | copy-start | bytes 49156
